TPU v7x, 256 devices: a whole 4x4x8 slice. The times are simulated.
256 devices in a mesh: pipe: 2 (over core), dp: 4 (over x), fsdp: 32 (over z, y).
Axes of the slice: x: 4, y: 4, z: 8, core: 2. Of those that a mesh axis runs over, the one named last changes fastest.
Arguments:
- incoming: bfloat16 [1024, 6144], P(('pipe', 'dp'), 'fsdp'), may hold values from -6 to 6
- cotangent: bfloat16 [1024, 6144], P(('pipe', 'dp'), 'fsdp'), may hold values from -6 to 6
- weights: bfloat16 [2, 3, 6144, 16384], P('pipe', None, 'dp', 'fsdp'), may hold values from -0.078125 to 0.078125
- token_rows: int32 [1024], P(('pipe', 'dp')), may hold values from 0 to 127, as said below
- row_count: int32 [8], P(('pipe', 'dp')), may hold values from 1 to 128, as said below
- gate: float32 [1024], P(('pipe', 'dp')), may hold values from 0.1 to 1
Outputs:
- d_input: bfloat16 [1024, 6144], P(('pipe', 'dp'), 'fsdp')
- weight_grad: bfloat16 [2, 3, 6144, 16384], P('pipe', None, 'dp', 'fsdp')
Inputs may be any that keep to these rules, and one draw needn't show every extreme that they name: `token_rows`: in each group the 128 entries are a permutation of 0 to 127; the first row_count entries name the tokens routed to the expert. `row_count`: some group's count is 128 in every draw.
All inputs are finite; a program needn't handle non-finite values.
Results may differ from a plain program's by a relative error of at most 0.02.
Values may be sent and summed in bfloat16 or wider, within the bound.
A program may use at most 128 MiB of HBM per device.

v0:
```python
import jax
import jax.numpy as jnp
from jax import lax
from jax.sharding import PartitionSpec as P


def from_behind(block, axis, distance):
    devices = range(lax.axis_size(axis))
    route = [((i - distance) % len(devices), i) for i in devices]
    return lax.ppermute(block, axis, route)


def on_device(incoming, cotangent, weights, token_rows, row_count, gate):
    panel = weights[0]
    hidden_local = panel.shape[2]
    tok_count = cotangent.shape[0]
    shifted = from_behind(incoming, "pipe", 1)
    arrived, returned = (
        lax.all_gather(shifted, "fsdp", axis=1, tiled=True),
        lax.all_gather(cotangent, "fsdp", axis=1, tiled=True),
    )
    full_width = arrived.shape[1]
    gathered = lax.all_gather(panel, "dp", axis=1, tiled=True)
    w_in = gathered[0:2]
    w_down = gathered[2]
    routed = jnp.take(arrived, token_rows, axis=0)
    pre = jnp.einsum("td,kdh->kth", routed, w_in, preferred_element_type=jnp.float32)
    gate_pre = pre[0]
    up_pre = pre[1]
    sigmoid_gate = jax.nn.sigmoid(gate_pre)
    activated = (gate_pre * sigmoid_gate * up_pre).astype(jnp.bfloat16)
    live = lax.broadcasted_iota(jnp.int32, (tok_count, 1), 0) < row_count[0]
    row_gates = jnp.take(gate, token_rows)[:, None]
    weighted = row_gates * jnp.take(returned, token_rows, axis=0).astype(jnp.float32)
    scaled = jnp.where(live, weighted, 0.0).astype(jnp.bfloat16)
    d_act = jnp.dot(scaled, w_down, preferred_element_type=jnp.float32)
    d_gate = d_act * up_pre * sigmoid_gate * (1.0 + gate_pre * (1.0 - sigmoid_gate))
    d_up = d_act * gate_pre * sigmoid_gate
    d_pre = jnp.concatenate([d_gate, d_up], axis=1).astype(jnp.bfloat16)
    d_routed = lax.dot_general(
        d_pre.reshape(tok_count, 2, hidden_local),
        w_in,
        (((1, 2), (0, 2)), ((), ())),
        preferred_element_type=jnp.float32,
    )
    terms = jnp.zeros((tok_count, full_width), jnp.float32).at[token_rows].set(d_routed)
    d_input = lax.psum_scatter(terms.astype(jnp.bfloat16), "fsdp", scatter_dimension=1, tiled=True)
    routed_cols, scaled_cols = (
        lax.all_to_all(routed, "dp", split_axis=1, concat_axis=0, tiled=True),
        lax.all_to_all(scaled, "dp", split_axis=1, concat_axis=0, tiled=True),
    )
    d_pre_piece = lax.all_gather(d_pre, "dp", axis=0, tiled=True)
    act_piece = lax.all_gather(activated, "dp", axis=0, tiled=True)
    inner = (((0,), (0,)), ((), ()))
    grad_in = lax.dot_general(routed_cols, d_pre_piece, inner, preferred_element_type=jnp.float32)
    grad_down = lax.dot_general(scaled_cols, act_piece, inner, preferred_element_type=jnp.float32)
    local_grad = jnp.stack([grad_in[:, :hidden_local], grad_in[:, hidden_local:], grad_down])
    return (d_input, local_grad.astype(jnp.bfloat16)[None])


def solution(mesh):
    return jax.shard_map(
        on_device,
        mesh=mesh,
        in_specs=(
            P(("pipe", "dp"), "fsdp"),
            P(("pipe", "dp"), "fsdp"),
            P("pipe", None, "dp", "fsdp"),
            P(("pipe", "dp")),
            P(("pipe", "dp")),
            P(("pipe", "dp")),
        ),
        out_specs=(P(("pipe", "dp"), "fsdp"), P("pipe", None, "dp", "fsdp")),
        check_vma=False,
    )
```

profile of v0, /device:TPU:4, one launch (start us, length us, event | category | flops | bytes accessed | tf_op | source)
XLA Modules:
  0.0 613.6 jit_solution(17832061655891211123)
XLA Ops:
  7.2 0.0 copy-start
  7.2 0.0 all-gather.6.cloned.1.call-start
  7.2 0.7 all-gather.6.cloned.1.call-update
  7.9 0.0 all-gather.8.cloned.1.call-start
  8.0 0.1 collective-permute-start
  8.1 1.4 collective-permute-done
  9.5 0.0 copy-start.4
  9.5 0.6 copy-done.4
  10.1 0.0 all-gather.8.cloned.1.call-update
  10.1 0.0 copy-start.5
  10.1 0.0 all-gather.12.cloned.1.call-start
  10.2 0.7 all-gather.12.cloned.1.call-update
  10.9 0.0 all-gather.10.cloned.1.call-start
  11.6 0.0 copy-done.5
  11.6 0.0 copy-done
  11.6 1.2 gather_fusion
  12.9 78.0 %all-gather.6.cloned.1.call-done = bf16[128,6144]{0,1:T(8,128)(2,1)} async-done(((bf16[128,192]{0,1:T(8,128)(2,1)}), bf16[128,6144]{0,1:T(8,128)(2,1)}) %all-gather.6.cloned.1.call-update) | async-done | bytes 1572880 | tf_op jit(solution)/shard_map/all_gather | solution.py:20
  90.8 1.7 copy.16
  92.6 1.5 gather_fusion.1
  94.1 0.7 select_convert_fusion
  94.8 73.9 %all-gather.8.cloned.1.call-done = bf16[128,6144]{0,1:T(8,128)(2,1)} async-done(((bf16[128,192]{0,1:T(8,128)(2,1)}), bf16[128,6144]{0,1:T(8,128)(2,1)}) %all-gather.8.cloned.1.call-update) | async-done | bytes 1572880 | tf_op jit(solution)/shard_map/all_gather | solution.py:19
  168.7 1.7 copy.17
  170.4 2.6 gather_fusion.2
  173.0 1.6 broadcast_select_fusion
  174.6 0.0 copy-start.2
  174.7 166.3 %all-gather.12.cloned.1.call-done = bf16[1,3,6144,512]{3,2,1,0:T(8,128)(2,1)} async-done(((bf16[1,3,1536,512]{3,2,1,0:T(8,128)(2,1)}), bf16[1,3,6144,512]{3,2,1,0:T(8,128)(2,1)}) %all-gather.12.cloned.1.call-update) | async-done | bytes 18874384 | tf_op jit(solution)/shard_map/all_gather | solution.py:23
  340.9 5.7 fusion.8
  346.6 0.0 copy-done.2
  346.7 3.9 multiply_convert_fusion.2
  350.6 0.8 pad_maximum_fusion.1
  351.4 0.0 all-gather.10.cloned.1.call-update
  351.4 1.3 copy.27
  352.7 5.5 all-to-all-start.1
  358.2 0.0 reduce-scatter.4.cloned.1.call-start
  358.2 10.4 %fusion.2 = f32[128,6144]{1,0:T(8,128)} fusion(bf16[1,3,6144,512]{3,2,1,0:T(8,128)(2,1)} %all-gather.12.cloned.1.call-done, bf16[128,1,512]{2,0,1:T(8,128)(2,1)S(1)} %bitcast.73, bf16[128,1,512]{2,0,1:T(8,128)(2,1)S(1)} %bitcast.72), kind=kOutput, calls=%fused_computation.7 | convolution fusion | flops 1610743808 | bytes 15990784 | tf_op jit(solution)/shard_map/dot_general | solution.py:40
  368.6 4.4 scatter_custom_fusion
  373.0 1.3 convert_element_type.24
  374.4 2.6 copy.21
  377.0 0.0 copy-start.3
  377.0 0.0 reduce-scatter.4.cloned.1.call-update
  377.0 1.4 copy-done.3
  378.4 1.3 copy.28
  379.7 4.9 all-to-all-done.1
  384.6 6.7 %all-to-all-start = ((bf16[128,4,1536]{2,0,1:T(8,128)(2,1)}), bf16[128,4,1536]{2,0,1:T(8,128)(2,1)S(1)}, u32[]{:S(2)}, u32[]{:S(2)}) async-start(bf16[128,4,1536]{2,0,1:T(8,128)(2,1)} %bitcast.65), calls=%async_computation | async-start | bytes 3145728 | tf_op jit(solution)/shard_map/all_to_all | solution.py:49
  391.3 26.2 %all_gather.19 = bf16[512,512]{1,0:T(8,128)(2,1)S(1)} all-gather(bf16[128,512]{1,0:T(8,128)(2,1)S(1)} %get-tuple-element.15), channel_id=1, replica_groups=mesh['pipe'=2,'dp'=4,'fsdp'=32] {'dp'}, dimensions={0}, use_global_device_ids=true | all-gather | bytes 655360 | tf_op jit(solution)/shard_map/all_gather | solution.py:53
  417.5 2.4 fusion.4
  419.9 0.0 all-to-all-done
  419.9 0.0 all-gather.10.cloned.1.call-done
  419.9 3.1 convolution_convert_fusion
  423.0 0.2 slice_bitcast_fusion.8
  423.3 0.0 copy-start.1
  423.3 2.5 pad_maximum_fusion
  425.7 181.3 %reduce-scatter.4.cloned.1.call-done = bf16[192,128]{1,0:T(8,128)(2,1)} async-done(((bf16[6144,128]{1,0:T(8,128)(2,1)}), bf16[192,128]{1,0:T(8,128)(2,1)}) %reduce-scatter.4.cloned.1.call-update) | async-done | bytes 49168
  607.0 0.0 copy-done.1
  (4 shorter events, 0.0 us)
Async XLA Ops:
  7.2 4.4 copy-start
  7.2 83.7 %all-gather.6.cloned.1.call-start = ((), (), s32[]{:S(2)}) async-start(), calls=%async_computation.3 | async-start | bytes 1622016 | tf_op jit(solution)/shard_map/all_gather | solution.py:20
  7.9 160.8 %all-gather.8.cloned.1.call-start = ((), (), s32[]{:S(2)}) async-start(), calls=%async_computation.4 | async-start | bytes 1622016 | tf_op jit(solution)/shard_map/all_gather | solution.py:19
  8.0 1.5 collective-permute-start
  9.5 0.6 copy-start.4
  10.1 1.4 copy-start.5
  10.1 330.8 %all-gather.12.cloned.1.call-start = ((), (), s32[]{:S(2)}) async-start(), calls=%async_computation.6 | async-start | bytes 23592960 | tf_op jit(solution)/shard_map/all_gather | solution.py:23
  10.9 409.0 %all-gather.10.cloned.1.call-start = ((), (), s32[]{:S(2)}) async-start(), calls=%async_computation.5 | async-start | bytes 1310720 | tf_op jit(solution)/shard_map/all_gather | solution.py:52
  174.6 172.0 %copy-start.2 = (bf16[128,6144]{1,0:T(8,128)(2,1)}, bf16[128,6144]{1,0:T(8,128)(2,1)S(1)}, u32[]{:S(2)}) copy-start(bf16[128,6144]{1,0:T(8,128)(2,1)S(1)} %broadcast_select_fusion) | copy-start | bytes 4718596
  352.7 31.9 %all-to-all-start.1 = ((bf16[128,4,1536]{2,0,1:T(8,128)(2,1)}), bf16[128,4,1536]{2,0,1:T(8,128)(2,1)}, u32[]{:S(2)}, u32[]{:S(2)}) async-start(bf16[128,4,1536]{2,0,1:T(8,128)(2,1)} %bitcast.64), calls=%async_computation.1 | async-start | bytes 3145728 | tf_op jit(solution)/shard_map/all_to_all | solution.py:50
  358.2 248.8 %reduce-scatter.4.cloned.1.call-start = ((), (), s32[]{:S(2)}) async-start(), calls=%async_computation.7 | async-start | bytes 1622016
  377.0 1.4 copy-start.3
  384.6 35.3 %all-to-all-start = ((bf16[128,4,1536]{2,0,1:T(8,128)(2,1)}), bf16[128,4,1536]{2,0,1:T(8,128)(2,1)S(1)}, u32[]{:S(2)}, u32[]{:S(2)}) async-start(bf16[128,4,1536]{2,0,1:T(8,128)(2,1)} %bitcast.65), calls=%async_computation | async-start | bytes 3145728 | tf_op jit(solution)/shard_map/all_to_all | solution.py:49
  423.3 183.8 %copy-start.1 = (f32[128]{0:T(128)S(1)}, f32[128]{0:T(128)}, u32[]{:S(2)}) copy-start(f32[128]{0:T(128)} %param.13) | copy-start | bytes 1540
Sparse Core Ops, SparseCore 0:
  10.6 80.1 all-gather.5
  94.0 74.6 all-gather.7
  170.5 170.3 all-gather.11
  351.5 33.5 all-gather.9
  389.3 217.6 reduce-scatter.3
where the time goes:
time: 614 us
  waiting for transfers between devices  507 us (83%)
  blocking collectives  26.2 us (4%)
  matrix products  25.5 us (4%)
  local copies, waits for them, and re-layouts  20.6 us (3%)
  between operations  14.6 us (2%)
  starting transfers between devices  12.5 us (2%)
  other arithmetic  6.93 us (1%)
    unnamed x6, waiting for transfers between devices  183 us
    all_gather x1, waiting for transfers between devices, on_device(): gathered = lax.all_gather(panel, 'dp', axis=1, tiled=True)  166 us
    all_gather x1, waiting for transfers between devices, on_device(): lax.all_gather(cotangent, 'fsdp', axis=1, tiled=True)  78 us
    all_gather x1, waiting for transfers between devices, on_device(): lax.all_gather(shifted, 'fsdp', axis=1, tiled=True)  73.9 us
    all_gather x1, blocking collectives, on_device(): act_piece = lax.all_gather(activated, 'dp', axis=0, tiled=True)  26.2 us
  transfers between devices with their start and end apart: 8, of which 6 were waited for; matrix products, arithmetic and copies ran while one was open for 7% of the time, Pallas kernels for 0%

commit v1 on v0

--- a/solution.py
+++ b/solution.py
@@ -2,6 +2,18 @@
 import jax.numpy as jnp
 from jax import lax
 from jax.sharding import PartitionSpec as P
+
+
+def collect(x, axis, dim):
+    ways, here, step = (lax.axis_size(axis), lax.axis_index(axis), x.shape[dim])
+    line, have = (x, 1)
+    while have < ways:
+        line = jnp.concatenate(
+            [line, lax.ppermute(line, axis, [(d, (d - have) % ways) for d in range(ways)])],
+            axis=dim,
+        )
+        have = 2 * have
+    return jnp.roll(line, here * step, axis=dim)
 
 
 def from_behind(block, axis, distance):
@@ -16,7 +28,7 @@
     tok_count = cotangent.shape[0]
     shifted = from_behind(incoming, "pipe", 1)
     arrived, returned = (
-        lax.all_gather(shifted, "fsdp", axis=1, tiled=True),
+        collect(shifted, "fsdp", 1),
         lax.all_gather(cotangent, "fsdp", axis=1, tiled=True),
     )
     full_width = arrived.shape[1]

time: 614 us -> 566 us (0.922)
  waiting for transfers between devices: 507 us -> 438 us
  starting transfers between devices: 12.5 us -> 26.5 us
    all_gather x1 -> x0, waiting for transfers between devices: 73.9 us -> none  [on_device(): lax.all_gather(shifted, 'fsdp', axis=1, tiled=True)]
    ppermute x0 -> x5, waiting for transfers between devices: none -> 60.9 us  [collect(): lax.ppermute(line, axis, [(d, (d - have) % ways) for d in range(ways)])]
    all_gather x1, waiting for transfers between devices: 78 us -> 22.7 us  [on_device(): lax.all_gather(cotangent, 'fsdp', axis=1, tiled=True)]
    ppermute x0 -> x5, starting transfers between devices: none -> 14.1 us  [collect(): lax.ppermute(line, axis, [(d, (d - have) % ways) for d in range(ways)])]
    unnamed x6 -> x5, waiting for transfers between devices: 183 us -> 183 us
  transfers between devices with their start and end apart: 8 -> 12, of which waited for: 6 -> 10; matrix products, arithmetic and copies ran while one was open for 7% -> 8% of each run, Pallas kernels for 0% -> 0%
where the time goes in v1:
time: 566 us; the launch traced here: 565 us
  waiting for transfers between devices  438 us (77%)
  starting transfers between devices  26.5 us (5%)
  blocking collectives  26.2 us (5%)
  local copies, waits for them, and re-layouts  25.6 us (5%)
  matrix products  25.5 us (5%)
  between operations  14.6 us (3%)
  other arithmetic  8.5 us (2%)
    unnamed x5, waiting for transfers between devices  183 us
    all_gather x1, waiting for transfers between devices, on_device(): gathered = lax.all_gather(panel, 'dp', axis=1, tiled=True)  166 us
    ppermute x5, waiting for transfers between devices, collect(): lax.ppermute(line, axis, [(d, (d - have) % ways) for d in range(ways)])  60.9 us
    all_gather x1, blocking collectives, on_device(): act_piece = lax.all_gather(activated, 'dp', axis=0, tiled=True)  26.2 us
    all_gather x1, waiting for transfers between devices, on_device(): lax.all_gather(cotangent, 'fsdp', axis=1, tiled=True)  22.7 us
    ppermute x5, starting transfers between devices, collect(): lax.ppermute(line, axis, [(d, (d - have) % ways) for d in range(ways)])  14.1 us
  transfers between devices with their start and end apart: 12, of which 10 were waited for; matrix products, arithmetic and copies ran while one was open for 8% of the time, Pallas kernels for 0%

profile of v1, /device:TPU:4, one launch (start us, length us, event | category | flops | bytes accessed | tf_op | source)
XLA Modules:
  0.0 565.2 jit_solution(1818755351479031315)
XLA Ops:
  7.2 0.0 copy-start
  7.2 0.0 all-gather.5.cloned.1.call-start
  7.2 0.7 all-gather.5.cloned.1.call-update
  7.9 0.0 copy-start.4
  7.9 0.0 all-gather.9.cloned.1.call-start
  8.0 0.7 all-gather.9.cloned.1.call-update
  8.7 0.0 all-gather.7.cloned.1.call-start
  8.7 0.0 copy-done.4
  8.7 0.1 copy.17
  8.8 0.0 copy-start.5
  8.9 0.1 collective-permute-start
  9.0 1.2 collective-permute-done
  10.2 8.3 %collective-permute-start.1 = (bf16[128,192]{1,0:T(8,128)(2,1)S(1)}, bf16[128,192]{1,0:T(8,128)(2,1)S(1)}, u32[]{:S(2)}, u32[]{:S(2)}) collective-permute-start(bf16[128,192]{1,0:T(8,128)(2,1)S(1)} %collective-permute-done), channel_id=1, source_target_pairs={{0,31},{1,0},{2,1},{3,2},{4,3},{5,4},{6,5},{7,6},{8,7},{9,8},{10,9... | collective-permute-start | bytes 147464 | tf_op jit(solution)/shard_map/ppermute | solution.py:12
  18.5 1.9 collective-permute-done.1
  20.4 0.1 pad_maximum_fusion.3
  20.5 2.6 collective-permute-start.2
  23.1 3.6 collective-permute-done.2
  26.7 0.1 pad_maximum_fusion.2
  26.8 1.1 collective-permute-start.3
  27.9 4.7 collective-permute-done.3
  32.6 0.1 concatenate.44
  32.7 1.8 collective-permute-start.4
  34.4 17.4 %collective-permute-done.4 = bf16[128,1536]{1,0:T(8,128)(2,1)S(1)} collective-permute-done((bf16[128,1536]{1,0:T(8,128)(2,1)S(1)}, bf16[128,1536]{1,0:T(8,128)(2,1)S(1)}, u32[]{:S(2)}, u32[]{:S(2)}) %collective-permute-start.4) | collective-permute-done | bytes 393248 | tf_op jit(solution)/shard_map/ppermute | solution.py:12
  51.9 0.3 concatenate.45
  52.1 0.3 collective-permute-start.5
  53.1 0.0 copy-done.5
  53.2 0.0 copy-done
  53.2 1.2 gather_fusion
  54.4 33.3 %collective-permute-done.5 = bf16[128,3072]{1,0:T(8,128)(2,1)S(1)} collective-permute-done((bf16[128,3072]{1,0:T(8,128)(2,1)S(1)}, bf16[128,3072]{1,0:T(8,128)(2,1)S(1)}, u32[]{:S(2)}, u32[]{:S(2)}) %collective-permute-start.5) | collective-permute-done | bytes 786464 | tf_op jit(solution)/shard_map/ppermute | solution.py:12
  87.8 3.6 concatenate.46
  91.4 2.0 constant_dynamic-slice_fusion
  93.4 2.6 gather_fusion.2
  96.0 1.6 broadcast_select_fusion
  97.7 22.7 %all-gather.5.cloned.1.call-done = bf16[128,6144]{0,1:T(8,128)(2,1)} async-done(((bf16[128,192]{0,1:T(8,128)(2,1)}), bf16[128,6144]{0,1:T(8,128)(2,1)}) %all-gather.5.cloned.1.call-update) | async-done | bytes 1572880 | tf_op jit(solution)/shard_map/all_gather | solution.py:32
  120.3 1.7 copy.16
  122.0 2.6 gather_fusion.1
  124.7 2.1 select_convert_fusion
  126.8 165.9 %all-gather.9.cloned.1.call-done = bf16[1,3,6144,512]{3,2,1,0:T(8,128)(2,1)} async-done(((bf16[1,3,1536,512]{3,2,1,0:T(8,128)(2,1)}), bf16[1,3,6144,512]{3,2,1,0:T(8,128)(2,1)}) %all-gather.9.cloned.1.call-update) | async-done | bytes 18874384 | tf_op jit(solution)/shard_map/all_gather | solution.py:35
  292.7 0.0 copy-done.2
  292.7 5.7 %fusion.8 = f32[2,128,512]{2,1,0:T(8,128)S(1)} fusion(bf16[1,3,6144,512]{3,2,1,0:T(8,128)(2,1)} %all-gather.9.cloned.1.call-done, bf16[128,6144]{1,0:T(8,128)(2,1)S(1)} %broadcast_select_fusion), kind=kOutput, calls=%fused_computation.23 | convolution fusion | flops 1610612736 | bytes 14680064 | tf_op jit(solution)/shard_map/td,kdh->kth/dot_general | solution.py:39
  298.3 3.9 multiply_convert_fusion.2
  302.3 0.8 pad_maximum_fusion.1
  303.1 0.0 all-gather.7.cloned.1.call-update
  303.1 1.3 copy.27
  304.4 5.5 all-to-all-start.1
  309.9 0.0 reduce-scatter.4.cloned.1.call-start
  309.9 10.4 %fusion.2 = f32[128,6144]{1,0:T(8,128)} fusion(bf16[1,3,6144,512]{3,2,1,0:T(8,128)(2,1)} %all-gather.9.cloned.1.call-done, bf16[128,1,512]{2,0,1:T(8,128)(2,1)S(1)} %bitcast.73, bf16[128,1,512]{2,0,1:T(8,128)(2,1)S(1)} %bitcast.72), kind=kOutput, calls=%fused_computation.7 | convolution fusion | flops 1610743808 | bytes 15990784 | tf_op jit(solution)/shard_map/dot_general | solution.py:52
  320.3 4.4 scatter_custom_fusion
  324.7 1.3 convert_element_type.24
  326.0 2.6 copy.21
  328.7 0.0 reduce-scatter.4.cloned.1.call-update
  328.7 1.4 copy-done.3
  330.1 1.3 copy.28
  331.4 4.9 all-to-all-done.1
  336.3 6.7 %all-to-all-start = ((bf16[128,4,1536]{2,0,1:T(8,128)(2,1)}), bf16[128,4,1536]{2,0,1:T(8,128)(2,1)S(1)}, u32[]{:S(2)}, u32[]{:S(2)}) async-start(bf16[128,4,1536]{2,0,1:T(8,128)(2,1)} %bitcast.65), calls=%async_computation | async-start | bytes 3145728 | tf_op jit(solution)/shard_map/all_to_all | solution.py:61
  343.0 26.2 %all_gather.15 = bf16[512,512]{1,0:T(8,128)(2,1)S(1)} all-gather(bf16[128,512]{1,0:T(8,128)(2,1)S(1)} %get-tuple-element.15), channel_id=1, replica_groups=mesh['pipe'=2,'dp'=4,'fsdp'=32] {'dp'}, dimensions={0}, use_global_device_ids=true | all-gather | bytes 655360 | tf_op jit(solution)/shard_map/all_gather | solution.py:65
  369.1 2.4 fusion.4
  371.6 0.0 all-to-all-done
  371.6 0.0 all-gather.7.cloned.1.call-done
  371.6 3.1 convolution_convert_fusion
  374.7 0.2 slice_bitcast_fusion.8
  374.9 0.0 copy-start.1
  374.9 2.5 pad_maximum_fusion
  377.4 181.2 %reduce-scatter.4.cloned.1.call-done = bf16[192,128]{1,0:T(8,128)(2,1)} async-done(((bf16[6144,128]{1,0:T(8,128)(2,1)}), bf16[192,128]{1,0:T(8,128)(2,1)}) %reduce-scatter.4.cloned.1.call-update) | async-done | bytes 49168
  (7 shorter events, 0.0 us)
Async XLA Ops:
  7.2 46.0 %copy-start = (f32[128]{0:T(128)S(1)}, f32[128]{0:T(128)}, u32[]{:S(2)}) copy-start(f32[128]{0:T(128)} %param.13) | copy-start | bytes 1540
  7.2 113.1 %all-gather.5.cloned.1.call-start = ((), (), s32[]{:S(2)}) async-start(), calls=%async_computation.3 | async-start | bytes 1622016 | tf_op jit(solution)/shard_map/all_gather | solution.py:32
  7.9 0.8 copy-start.4
  7.9 284.7 %all-gather.9.cloned.1.call-start = ((), (), s32[]{:S(2)}) async-start(), calls=%async_computation.5 | async-start | bytes 23592960 | tf_op jit(solution)/shard_map/all_gather | solution.py:35
  8.7 362.9 %all-gather.7.cloned.1.call-start = ((), (), s32[]{:S(2)}) async-start(), calls=%async_computation.4 | async-start | bytes 1310720 | tf_op jit(solution)/shard_map/all_gather | solution.py:64
  8.8 44.3 %copy-start.5 = (s32[128]{0:T(128)S(1)}, s32[128]{0:T(128)}, u32[]{:S(2)}) copy-start(s32[128]{0:T(128)} %param.11) | copy-start | bytes 1540
  8.9 1.3 collective-permute-start
  10.2 10.2 %collective-permute-start.1 = (bf16[128,192]{1,0:T(8,128)(2,1)S(1)}, bf16[128,192]{1,0:T(8,128)(2,1)S(1)}, u32[]{:S(2)}, u32[]{:S(2)}) collective-permute-start(bf16[128,192]{1,0:T(8,128)(2,1)S(1)} %collective-permute-done), channel_id=1, source_target_pairs={{0,31},{1,0},{2,1},{3,2},{4,3},{5,4},{6,5},{7,6},{8,7},{9,8},{10,9... | collective-permute-start | bytes 147464 | tf_op jit(solution)/shard_map/ppermute | solution.py:12
  20.5 6.2 %collective-permute-start.2 = (bf16[128,384]{1,0:T(8,128)(2,1)S(1)}, bf16[128,384]{1,0:T(8,128)(2,1)S(1)}, u32[]{:S(2)}, u32[]{:S(2)}) collective-permute-start(bf16[128,384]{1,0:T(8,128)(2,1)S(1)} %pad_maximum_fusion.3), channel_id=1, source_target_pairs={{0,30},{1,31},{2,0},{3,1},{4,2},{5,3},{6,4},{7,5},{8,6},{9,7},{10,... | collective-permute-start | bytes 294920 | tf_op jit(solution)/shard_map/ppermute | solution.py:12
  26.8 5.8 %collective-permute-start.3 = (bf16[128,768]{1,0:T(8,128)(2,1)S(1)}, bf16[128,768]{1,0:T(8,128)(2,1)S(1)}, u32[]{:S(2)}, u32[]{:S(2)}) collective-permute-start(bf16[128,768]{1,0:T(8,128)(2,1)S(1)} %pad_maximum_fusion.2), channel_id=1, source_target_pairs={{0,28},{1,29},{2,30},{3,31},{4,0},{5,1},{6,2},{7,3},{8,4},{9,5},{1... | collective-permute-start | bytes 589832 | tf_op jit(solution)/shard_map/ppermute | solution.py:12
  32.7 19.2 %collective-permute-start.4 = (bf16[128,1536]{1,0:T(8,128)(2,1)S(1)}, bf16[128,1536]{1,0:T(8,128)(2,1)S(1)}, u32[]{:S(2)}, u32[]{:S(2)}) collective-permute-start(bf16[128,1536]{1,0:T(8,128)(2,1)S(1)} %concatenate.44), channel_id=1, source_target_pairs={{0,24},{1,25},{2,26},{3,27},{4,28},{5,29},{6,30},{7,31},{8,0},{9,1... | collective-permute-start | bytes 1179656 | tf_op jit(solution)/shard_map/ppermute | solution.py:12
  52.1 35.6 %collective-permute-start.5 = (bf16[128,3072]{1,0:T(8,128)(2,1)S(1)}, bf16[128,3072]{1,0:T(8,128)(2,1)S(1)}, u32[]{:S(2)}, u32[]{:S(2)}) collective-permute-start(bf16[128,3072]{1,0:T(8,128)(2,1)S(1)} %concatenate.45), channel_id=1, source_target_pairs={{0,16},{1,17},{2,18},{3,19},{4,20},{5,21},{6,22},{7,23},{8,24},{9,... | collective-permute-start | bytes 2359304 | tf_op jit(solution)/shard_map/ppermute | solution.py:12
  97.6 195.0 %copy-start.2 = (bf16[128,6144]{1,0:T(8,128)(2,1)}, bf16[128,6144]{1,0:T(8,128)(2,1)S(1)}, u32[]{:S(2)}) copy-start(bf16[128,6144]{1,0:T(8,128)(2,1)S(1)} %broadcast_select_fusion) | copy-start | bytes 4718596
  304.4 31.9 %all-to-all-start.1 = ((bf16[128,4,1536]{2,0,1:T(8,128)(2,1)}), bf16[128,4,1536]{2,0,1:T(8,128)(2,1)}, u32[]{:S(2)}, u32[]{:S(2)}) async-start(bf16[128,4,1536]{2,0,1:T(8,128)(2,1)} %bitcast.64), calls=%async_computation.1 | async-start | bytes 3145728 | tf_op jit(solution)/shard_map/all_to_all | solution.py:62
  309.9 248.7 %reduce-scatter.4.cloned.1.call-start = ((), (), s32[]{:S(2)}) async-start(), calls=%async_computation.6 | async-start | bytes 1622016
  328.7 1.4 copy-start.3
  336.3 35.3 %all-to-all-start = ((bf16[128,4,1536]{2,0,1:T(8,128)(2,1)}), bf16[128,4,1536]{2,0,1:T(8,128)(2,1)S(1)}, u32[]{:S(2)}, u32[]{:S(2)}) async-start(bf16[128,4,1536]{2,0,1:T(8,128)(2,1)} %bitcast.65), calls=%async_computation | async-start | bytes 3145728 | tf_op jit(solution)/shard_map/all_to_all | solution.py:61
  374.9 183.7 %copy-start.1 = (f32[128]{0:T(128)S(1)}, f32[128]{0:T(128)}, u32[]{:S(2)}) copy-start(f32[128]{0:T(128)} %param.13) | copy-start | bytes 1540
Sparse Core Ops, SparseCore 0:
  10.6 109.6 all-gather.4
  122.2 170.4 all-gather.8
  303.2 33.5 all-gather.6
  341.0 217.5 reduce-scatter.3
